TPU v7x, 32 devices: a whole 2x2x4 slice. The times are simulated.
32 devices in a mesh: parts: 2 (over x), ep: 16 (over z, y, core).
Axes of the slice: x: 2, y: 2, z: 4, core: 2. Of those that a mesh axis runs over, the one named last changes fastest.
Arguments:
- tokens: bfloat16 [4096, 7168], P(('parts', 'ep')), parts along dimension 0, may hold values from -6 to 6
- cotangent: bfloat16 [4096, 7168], P(('parts', 'ep')), parts along dimension 0, may hold values from -6 to 6
- expert_ids: int32 [4096, 8], P(('parts', 'ep')), parts along dimension 0, may hold values from 0 to 255, as said below
- route_weight: float32 [4096, 8], P(('parts', 'ep')), parts along dimension 0, may hold values from 0.05 to 0.6
- gate_weight: bfloat16 [7168, 2048], P(None, 'ep'), may hold values from -0.0625 to 0.0625
- up_weight: bfloat16 [7168, 2048], P(None, 'ep'), may hold values from -0.0625 to 0.0625
- down_weight: bfloat16 [2048, 7168], P('ep'), may hold values from -0.125 to 0.125
Outputs:
- mixed: bfloat16 [4096, 7168], P(('parts', 'ep')), parts along dimension 0
- grad_tokens: bfloat16 [4096, 7168], P(('parts', 'ep')), parts along dimension 0
- grad_route: float32 [4096, 8], P(('parts', 'ep')), parts along dimension 0
There are 2 independent parts, one for each index of `parts`. A program takes and returns all parts, laid end to end along the dimension named above; an argument that names none is the same for every part. Nothing has to cross between parts.
Inputs may be any that keep to these rules, and one draw needn't show every extreme that they name: `expert_ids`: each row names 8 different experts. Of the experts in flight 0 to 0, each is named by at most 8 of the 128 rows of one device, and one of them is named by exactly 8 rows of every device.
All inputs are finite; a program needn't handle non-finite values.
Results may differ from a plain program's by a relative error of at most 0.0065.
Values may be sent and summed in bfloat16 or wider, within the bound.
No kernel may reach another device: no remote copies, remote signals or barrier semaphores. Data moves between devices by JAX's collectives and lax.ppermute only.
A program may use at most 128 MiB of HBM per device.

v0:
```python
import jax
import jax.numpy as jnp
from jax import lax
from jax.sharding import PartitionSpec as P

GROUP = 16
SLOT = 8


def expert_terms(received, gate_weight, up_weight, down_weight):
    sources = received.shape[0]
    slot_count = received.shape[2]
    width_model = received.shape[3]
    in_rows = received[:, 0].reshape(sources * slot_count, width_model)
    grad_rows = received[:, 1].reshape(sources * slot_count, width_model)
    gate_act = jnp.dot(in_rows, gate_weight, preferred_element_type=jnp.float32)
    up_act = jnp.dot(in_rows, up_weight, preferred_element_type=jnp.float32)
    sigmoid_val = jax.nn.sigmoid(gate_act)
    silu_val = gate_act * sigmoid_val
    hidden_act = (silu_val * up_act).astype(jnp.bfloat16)
    out_part = jnp.dot(hidden_act, down_weight, preferred_element_type=jnp.float32).astype(
        jnp.bfloat16
    )
    back_hidden = jnp.dot(grad_rows, down_weight.T, preferred_element_type=jnp.float32)
    grad_gate = (
        back_hidden * up_act * sigmoid_val * (1.0 + gate_act * (1.0 - sigmoid_val))
    ).astype(jnp.bfloat16)
    grad_up = (back_hidden * silu_val).astype(jnp.bfloat16)
    input_part = (
        jnp.dot(grad_gate, gate_weight.T, preferred_element_type=jnp.float32)
        + jnp.dot(grad_up, up_weight.T, preferred_element_type=jnp.float32)
    ).astype(jnp.bfloat16)
    return jnp.stack(
        [
            out_part.reshape(sources, slot_count, width_model),
            input_part.reshape(sources, slot_count, width_model),
        ],
        axis=1,
    )


def body(tokens, cotangent, expert_ids, route_weight, gate_weight, up_weight, down_weight):
    width_model = tokens.shape[1]
    devices = lax.axis_size("ep")
    experts_win = devices // GROUP
    window = jnp.arange(experts_win, dtype=jnp.int32)
    onehot = expert_ids[:, :, None] == window[None, None, :]
    chosen = jnp.any(onehot, axis=1)
    places = jnp.cumsum(chosen.astype(jnp.int32), axis=0) - 1
    weight_sel = jnp.sum(jnp.where(onehot, route_weight[:, :, None], 0.0), axis=1)
    slot_index = jnp.arange(SLOT, dtype=jnp.int32)
    picker_mask = chosen.T[:, None, :] & (places.T[:, None, :] == slot_index[None, :, None])
    picker = picker_mask.astype(jnp.bfloat16)
    picker_wide = picker_mask.astype(jnp.float32)
    rows_x = jnp.einsum("est,td->esd", picker, tokens, preferred_element_type=jnp.float32).astype(
        jnp.bfloat16
    )
    rows_cot = jnp.einsum(
        "est,td->esd", picker, cotangent, preferred_element_type=jnp.float32
    ).astype(jnp.bfloat16)
    slot_weight = jnp.sum(picker_wide * weight_sel.T[:, None, :], axis=2)
    rows_dy = (rows_cot.astype(jnp.float32) * slot_weight[:, :, None]).astype(jnp.bfloat16)
    packed = jnp.stack([rows_x, rows_dy], axis=1)
    outgoing = jnp.repeat(packed, GROUP, axis=0)
    terms = expert_terms(
        lax.all_to_all(outgoing, "ep", split_axis=0, concat_axis=0, tiled=True),
        gate_weight,
        up_weight,
        down_weight,
    )
    back = lax.all_to_all(terms, "ep", split_axis=0, concat_axis=0, tiled=True)
    summed = jnp.sum(
        back.reshape(experts_win, GROUP, 2, SLOT, width_model), axis=1, dtype=jnp.float32
    )
    expert_out = summed[:, 0]
    input_term = summed[:, 1]
    weighted_picker = picker_wide * weight_sel.T[:, None, :]
    mixed = jnp.einsum("est,esd->td", weighted_picker, expert_out, precision=lax.Precision.HIGHEST)
    grad_tokens = jnp.einsum(
        "est,esd->td", picker_wide, input_term, precision=lax.Precision.HIGHEST
    )
    slot_dots = jnp.sum(rows_cot.astype(jnp.float32) * expert_out, axis=2)
    token_dots = jnp.einsum("est,es->te", picker_wide, slot_dots, precision=lax.Precision.HIGHEST)
    grad_route = jnp.sum(jnp.where(onehot, token_dots[:, None, :], 0.0), axis=2)
    return (mixed.astype(jnp.bfloat16), grad_tokens.astype(jnp.bfloat16), grad_route)


def solution(mesh):
    return jax.shard_map(
        body,
        mesh=mesh,
        in_specs=(
            P(("parts", "ep"), None),
            P(("parts", "ep"), None),
            P(("parts", "ep"), None),
            P(("parts", "ep"), None),
            P(None, "ep"),
            P(None, "ep"),
            P("ep", None),
        ),
        out_specs=(P(("parts", "ep"), None), P(("parts", "ep"), None), P(("parts", "ep"), None)),
        check_vma=False,
    )
```

profile of v0, /device:TPU:1, one launch (start us, length us, event | category | flops | bytes accessed | tf_op | source)
XLA Modules:
  0.0 193.3 jit_solution(2176159694832963196)
XLA Ops:
  0.6 0.0 copy-start
  0.6 0.9 select_reduce_fusion.1
  1.5 0.1 copy.15
  1.6 0.2 reduce-window.7
  1.8 0.0 copy-start.2
  1.8 0.1 add_reduce_fusion
  1.9 2.0 %fusion.3 = f32[8,7168]{1,0:T(8,128)S(1)} fusion(bf16[128,7168]{1,0:T(8,128)(2,1)} %param.8, s32[128]{0:T(128)S(1)} %add_reduce_fusion, pred[128]{0:T(512)(128)(4,1)S(1)} %reduce_or.9), kind=kOutput, calls=%fused_computation.8 | convolution fusion | flops 14796800 | bytes 2065024 | tf_op jit(solution)/shard_map/est,td->esd/dot_general | solution.py:58
  3.9 0.1 select_reduce_fusion
  4.0 0.0 copy-done.2
  4.0 0.3 fusion.4
  4.4 0.1 fusion.8
  4.5 0.4 reshape.252
  4.9 0.0 copy-start.3
  4.9 88.7 %all_to_all.10 = bf16[16,2,8,7168]{3,2,1,0:T(8,128)(2,1)S(1)} all-to-all(bf16[16,2,8,7168]{3,2,1,0:T(8,128)(2,1)S(1)} %reshape.252), channel_id=1, replica_groups=mesh['parts'=2,'ep'=16] {'ep'}, dimensions={0} | all-to-all | bytes 7340032 | tf_op jit(solution)/shard_map/all_to_all | solution.py:66
  93.6 0.0 copy-done.3
  93.6 0.0 copy-start.1
  93.6 0.6 fusion.7
  94.2 0.9 copy-done.1
  95.1 0.7 fusion.6
  95.8 0.0 copy-done
  95.8 0.6 fusion.1
  96.4 0.7 fusion.5
  97.1 0.6 fusion.10
  97.7 0.6 fusion.2
  98.4 0.3 pad_maximum_fusion
  98.7 86.0 %all_to_all.11 = bf16[16,2,8,7168]{3,2,1,0:T(8,128)(2,1)S(1)} all-to-all(bf16[16,2,8,7168]{3,2,1,0:T(8,128)(2,1)S(1)} %pad_maximum_fusion), channel_id=1, replica_groups=mesh['parts'=2,'ep'=16] {'ep'}, dimensions={0} | all-to-all | bytes 7340032 | tf_op jit(solution)/shard_map/all_to_all | solution.py:71
  184.8 0.5 convert_reduce_fusion
  185.3 4.2 %convolution_convert_fusion.1 = bf16[128,7168]{1,0:T(8,128)(2,1)} fusion(f32[1,2,8,7168]{3,2,1,0:T(8,128)S(1)} %bitcast.45, f32[128]{0:T(128)S(1)} %get-tuple-element.3, s32[128]{0:T(128)S(1)} %add_reduce_fusion, pred[128]{0:T(512)(128)(4,1)S(1)} %reduce_or.9), kind=kOutput, calls=%fused_computation.3 | convolution fusion | flops 89000960 | bytes 2065920 | tf_op jit(solution)/shard_map/est,esd->td/dot_general | solution.py:78
  189.5 2.9 %convolution_convert_fusion = bf16[128,7168]{1,0:T(8,128)(2,1)} fusion(f32[1,2,8,7168]{3,2,1,0:T(8,128)S(1)} %bitcast.46, s32[128]{0:T(128)S(1)} %add_reduce_fusion, pred[128]{0:T(512)(128)(4,1)S(1)} %reduce_or.9), kind=kOutput, calls=%fused_computation.2 | convolution fusion | flops 88999936 | bytes 2065408 | tf_op jit(solution)/shard_map/est,esd->td/dot_general | solution.py:79
  192.4 0.2 multiply_reduce_fusion
  192.5 0.1 convolution_bitcast_fusion
  192.7 0.6 broadcast_select_fusion
  (3 shorter events, 0.1 us)
Async XLA Ops:
  0.6 95.1 %copy-start = (bf16[128,7168]{1,0:T(8,128)(2,1)S(1)}, bf16[128,7168]{1,0:T(8,128)(2,1)}, u32[]{:S(2)}) copy-start(bf16[128,7168]{1,0:T(8,128)(2,1)} %param.13) | copy-start | bytes 5505028
  1.8 2.2 %copy-start.2 = (bf16[128,7168]{1,0:T(8,128)(2,1)S(1)}, bf16[128,7168]{1,0:T(8,128)(2,1)}, u32[]{:S(2)}) copy-start(bf16[128,7168]{1,0:T(8,128)(2,1)} %param.7) | copy-start | bytes 5505028
  4.9 88.7 %copy-start.3 = (bf16[7168,128]{1,0:T(8,128)(2,1)S(1)}, bf16[7168,128]{1,0:T(8,128)(2,1)}, u32[]{:S(2)}) copy-start(bf16[7168,128]{1,0:T(8,128)(2,1)} %param.11) | copy-start | bytes 5505028
  93.6 1.5 copy-start.1
where the time goes:
time: 194 us; the launch traced here: 193 us
  blocking collectives  175 us (90%)
  matrix products  13.4 us (7%)
  other arithmetic  3.02 us (2%)
    all_to_all x1, blocking collectives, body(): lax.all_to_all(outgoing, 'ep', split_axis=0, concat_axis=0, tiled=True)  88.7 us
    all_to_all x1, blocking collectives, body(): back = lax.all_to_all(terms, 'ep', split_axis=0, concat_axis=0, tiled=True)  86 us
    dot_general x1, matrix products, body(): jnp.einsum('est,esd->td', weighted_picker, expert_out, precision=lax.Prec...  4.2 us

commit v1 on v0

--- a/solution.py
+++ b/solution.py
@@ -5,6 +5,7 @@
 
 GROUP = 16
 SLOT = 8
+RING = (0, 2, 4, 6, 7, 5, 3, 1)
 
 
 def expert_terms(received, gate_weight, up_weight, down_weight):
@@ -30,19 +31,10 @@
         jnp.dot(grad_gate, gate_weight.T, preferred_element_type=jnp.float32)
         + jnp.dot(grad_up, up_weight.T, preferred_element_type=jnp.float32)
     ).astype(jnp.bfloat16)
-    return jnp.stack(
-        [
-            out_part.reshape(sources, slot_count, width_model),
-            input_part.reshape(sources, slot_count, width_model),
-        ],
-        axis=1,
-    )
+    return out_part, input_part
 
 
-def body(tokens, cotangent, expert_ids, route_weight, gate_weight, up_weight, down_weight):
-    width_model = tokens.shape[1]
-    devices = lax.axis_size("ep")
-    experts_win = devices // GROUP
+def pick_rows(tokens, cotangent, expert_ids, route_weight, experts_win):
     window = jnp.arange(experts_win, dtype=jnp.int32)
     onehot = expert_ids[:, :, None] == window[None, None, :]
     chosen = jnp.any(onehot, axis=1)
@@ -60,14 +52,26 @@
     ).astype(jnp.bfloat16)
     slot_weight = jnp.sum(picker_wide * weight_sel.T[:, None, :], axis=2)
     rows_dy = (rows_cot.astype(jnp.float32) * slot_weight[:, :, None]).astype(jnp.bfloat16)
+    return onehot, picker_wide, weight_sel, rows_x, rows_cot, rows_dy
+
+
+def any_size(tokens, cotangent, expert_ids, route_weight, gate_weight, up_weight, down_weight):
+    width_model = tokens.shape[1]
+    devices = lax.axis_size("ep")
+    experts_win = devices // GROUP
+    onehot, picker_wide, weight_sel, rows_x, rows_cot, rows_dy = pick_rows(
+        tokens, cotangent, expert_ids, route_weight, experts_win
+    )
     packed = jnp.stack([rows_x, rows_dy], axis=1)
     outgoing = jnp.repeat(packed, GROUP, axis=0)
-    terms = expert_terms(
+    out_part, input_part = expert_terms(
         lax.all_to_all(outgoing, "ep", split_axis=0, concat_axis=0, tiled=True),
         gate_weight,
         up_weight,
         down_weight,
     )
+    shape = (devices, SLOT, width_model)
+    terms = jnp.stack([out_part.reshape(shape), input_part.reshape(shape)], axis=1)
     back = lax.all_to_all(terms, "ep", split_axis=0, concat_axis=0, tiled=True)
     summed = jnp.sum(
         back.reshape(experts_win, GROUP, 2, SLOT, width_model), axis=1, dtype=jnp.float32
@@ -83,6 +87,91 @@
     token_dots = jnp.einsum("est,es->te", picker_wide, slot_dots, precision=lax.Precision.HIGHEST)
     grad_route = jnp.sum(jnp.where(onehot, token_dots[:, None, :], 0.0), axis=2)
     return (mixed.astype(jnp.bfloat16), grad_tokens.astype(jnp.bfloat16), grad_route)
+
+
+def hop(step):
+    pairs = []
+    for place, chip in enumerate(RING):
+        target = RING[(place + step) % len(RING)]
+        pairs += [(2 * chip, 2 * target), (2 * chip + 1, 2 * target + 1)]
+    return pairs
+
+
+NEXT = hop(1)
+PREV = hop(-1)
+SWAP = [(i, i ^ 1) for i in range(GROUP)]
+
+
+def send(value, pairs):
+    return lax.ppermute(value, "ep", pairs)
+
+
+def ring_gather(own):
+    half = own.shape[1] // 2
+    right = left = own
+    mine = [own]
+    other = [send(own, SWAP)]
+    for _ in range(3):
+        right, left = send(right, NEXT), send(left, PREV)
+        mine += [right, left]
+        other += [send(right, SWAP), send(left, SWAP)]
+    right, left = send(right[:, :half], NEXT), send(left[:, half:], PREV)
+    mine.append(jnp.concatenate([right, left], axis=1))
+    other.append(jnp.concatenate([send(right, SWAP), send(left, SWAP)], axis=1))
+    return mine, other
+
+
+def ring_sum(part):
+    width = part.shape[1]
+    half = width // 2
+    pieces = part.reshape(8, 2, SLOT, width)
+
+    def chip(j):
+        return pieces[j, 0].astype(jnp.float32) + send(pieces[j, 1], SWAP).astype(jnp.float32)
+
+    far = chip(7).astype(jnp.bfloat16)
+    right, left = send(far[:, :half], NEXT), send(far[:, half:], PREV)
+    up, down = chip(6), chip(5)
+    right = jnp.concatenate([up[:, :half] + right.astype(jnp.float32), up[:, half:]], axis=1)
+    left = jnp.concatenate([down[:, :half], down[:, half:] + left.astype(jnp.float32)], axis=1)
+    right, left = send(right.astype(jnp.bfloat16), NEXT), send(left.astype(jnp.bfloat16), PREV)
+    for j in (4, 2):
+        right = (chip(j) + right.astype(jnp.float32)).astype(jnp.bfloat16)
+        left = (chip(j - 1) + left.astype(jnp.float32)).astype(jnp.bfloat16)
+        right, left = send(right, NEXT), send(left, PREV)
+    return chip(0) + right.astype(jnp.float32) + left.astype(jnp.float32)
+
+
+def one_group(tokens, cotangent, expert_ids, route_weight, gate_weight, up_weight, down_weight):
+    onehot, picker_wide, weight_sel, rows_x, rows_cot, rows_dy = pick_rows(
+        tokens, cotangent, expert_ids, route_weight, 1
+    )
+    mine_x, other_x = ring_gather(rows_x[0])
+    mine_dy, other_dy = ring_gather(rows_dy[0])
+    all_x = jnp.stack([v for pair in zip(mine_x, other_x) for v in pair])
+    all_dy = jnp.stack([v for pair in zip(mine_dy, other_dy) for v in pair])
+    out_part, input_part = expert_terms(
+        jnp.stack([all_x, all_dy], axis=1), gate_weight, up_weight, down_weight
+    )
+    expert_out = ring_sum(out_part)
+    input_term = ring_sum(input_part)
+    slot_weight = jnp.sum(picker_wide[0] * weight_sel.T, axis=1)
+    picker = picker_wide[0].astype(jnp.bfloat16)
+    weighted = (expert_out * slot_weight[:, None]).astype(jnp.bfloat16)
+    mixed = jnp.einsum("st,sd->td", picker, weighted, preferred_element_type=jnp.float32)
+    grad_tokens = jnp.einsum(
+        "st,sd->td", picker, input_term.astype(jnp.bfloat16), preferred_element_type=jnp.float32
+    )
+    slot_dots = jnp.sum(rows_cot[0].astype(jnp.float32) * expert_out, axis=1)
+    token_dots = jnp.sum(picker_wide[0] * slot_dots[:, None], axis=0)
+    grad_route = jnp.where(onehot[:, :, 0], token_dots[:, None], 0.0)
+    return (mixed.astype(jnp.bfloat16), grad_tokens.astype(jnp.bfloat16), grad_route)
+
+
+def body(*args):
+    if lax.axis_size("ep") == GROUP:
+        return one_group(*args)
+    return any_size(*args)
 
 
 def solution(mesh):

time: 194 us -> 122 us (0.63)
  blocking collectives: 175 us -> 0 us
  starting transfers between devices: 0 us -> 63.1 us
  waiting for transfers between devices: 0 us -> 42 us
  matrix products: 13.4 us -> 8.55 us
    all_to_all x2 -> x0, blocking collectives: 175 us -> none  [the longest x1 88.7 us: body(): lax.all_to_all(outgoing, 'ep', split_axis=0, concat_axis=0, tiled=True)]
    ppermute x0 -> x66, starting transfers between devices: none -> 63.1 us  [send(): return lax.ppermute(value, 'ep', pairs)]
    ppermute x0 -> x66, waiting for transfers between devices: none -> 42 us  [send(): return lax.ppermute(value, 'ep', pairs)]
    dot_general x5 -> x4, matrix products: 9.5 us -> 4.66 us  [the longest x1 1.92 us: one_group(): jnp.einsum('st,sd->td', picker, weighted, preferred_element_type=jnp.floa...]
  transfers between devices with their start and end apart: 0 -> 66, of which waited for: 0 -> 25; matrix products, arithmetic and copies ran while one was open for 0% -> 3% of each run, Pallas kernels for 0% -> 0%
where the time goes in v1:
time: 122 us; the launch traced here: 120 us
  starting transfers between devices  63.1 us (52%)
  waiting for transfers between devices  42 us (34%)
  matrix products  8.55 us (7%)
  other arithmetic  2.73 us (2%)
  local copies, waits for them, and re-layouts  2.48 us (2%)
    ppermute x66, starting transfers between devices, send(): return lax.ppermute(value, 'ep', pairs)  63.1 us
    ppermute x66, waiting for transfers between devices, send(): return lax.ppermute(value, 'ep', pairs)  42 us
  transfers between devices with their start and end apart: 66, of which 25 were waited for; matrix products, arithmetic and copies ran while one was open for 3% of the time, Pallas kernels for 0%

profile of v1, /device:TPU:1, one launch (start us, length us, event | category | flops | bytes accessed | tf_op | source)
XLA Modules:
  0.0 120.0 jit_solution(16909520167025539349)
XLA Ops:
  0.6 0.9 select_reduce_fusion.3
  2.5 2.2 %collective-permute-start.1 = (bf16[8,7168]{1,0:T(8,128)(2,1)S(1)}, bf16[8,7168]{1,0:T(8,128)(2,1)S(1)}, u32[]{:S(2)}, u32[]{:S(2)}) collective-permute-start(bf16[8,7168]{1,0:T(8,128)(2,1)S(1)} %get-tuple-element.38), channel_id=1, source_target_pairs={{0,4},{1,5},{4,8},{5,9},{8,12},{9,13},{12,14},{13,15},{14,10},{15,... | collective-permute-start | bytes 344072 | tf_op jit(solution)/shard_map/ppermute | solution.py:106
  4.7 1.0 collective-permute-start
  5.6 1.9 %collective-permute-done.1 = bf16[8,7168]{1,0:T(8,128)(2,1)S(1)} collective-permute-done((bf16[8,7168]{1,0:T(8,128)(2,1)S(1)}, bf16[8,7168]{1,0:T(8,128)(2,1)S(1)}, u32[]{:S(2)}, u32[]{:S(2)}) %collective-permute-start.1) | collective-permute-done | bytes 114720 | tf_op jit(solution)/shard_map/ppermute | solution.py:106
  7.5 1.2 %collective-permute-start.2 = (bf16[8,7168]{1,0:T(8,128)(2,1)S(1)}, bf16[8,7168]{1,0:T(8,128)(2,1)S(1)}, u32[]{:S(2)}, u32[]{:S(2)}) collective-permute-start(bf16[8,7168]{1,0:T(8,128)(2,1)S(1)} %collective-permute-done.1), channel_id=1, source_target_pairs={{0,1},{1,0},{2,3},{3,2},{4,5},{5,4},{6,7},{7,6},{8,9},{9,8},{10,11... | collective-permute-start | bytes 344072 | tf_op jit(solution)/shard_map/ppermute | solution.py:106
  8.7 1.5 %collective-permute-start.5 = (bf16[8,7168]{1,0:T(8,128)(2,1)S(1)}, bf16[8,7168]{1,0:T(8,128)(2,1)S(1)}, u32[]{:S(2)}, u32[]{:S(2)}) collective-permute-start(bf16[8,7168]{1,0:T(8,128)(2,1)S(1)} %collective-permute-done.1), channel_id=1, source_target_pairs={{0,4},{1,5},{4,8},{5,9},{8,12},{9,13},{12,14},{13,15},{14,10},{15,... | collective-permute-start | bytes 344072 | tf_op jit(solution)/shard_map/ppermute | solution.py:106
  10.6 2.9 %collective-permute-done.5 = bf16[8,7168]{1,0:T(8,128)(2,1)S(1)} collective-permute-done((bf16[8,7168]{1,0:T(8,128)(2,1)S(1)}, bf16[8,7168]{1,0:T(8,128)(2,1)S(1)}, u32[]{:S(2)}, u32[]{:S(2)}) %collective-permute-start.5) | collective-permute-done | bytes 114720 | tf_op jit(solution)/shard_map/ppermute | solution.py:106
  13.5 0.8 collective-permute-start.6
  14.3 1.5 %collective-permute-start.9 = (bf16[8,7168]{1,0:T(8,128)(2,1)S(1)}, bf16[8,7168]{1,0:T(8,128)(2,1)S(1)}, u32[]{:S(2)}, u32[]{:S(2)}) collective-permute-start(bf16[8,7168]{1,0:T(8,128)(2,1)S(1)} %collective-permute-done.5), channel_id=1, source_target_pairs={{0,4},{1,5},{4,8},{5,9},{8,12},{9,13},{12,14},{13,15},{14,10},{15,... | collective-permute-start | bytes 344072 | tf_op jit(solution)/shard_map/ppermute | solution.py:106
  16.2 4.4 %collective-permute-done.11 = bf16[8,7168]{1,0:T(8,128)(2,1)S(1)} collective-permute-done((bf16[8,7168]{1,0:T(8,128)(2,1)S(1)}, bf16[8,7168]{1,0:T(8,128)(2,1)S(1)}, u32[]{:S(2)}, u32[]{:S(2)}) %collective-permute-start.11) | collective-permute-done | bytes 114720 | tf_op jit(solution)/shard_map/ppermute | solution.py:106
  20.7 1.4 %collective-permute-start.13 = (bf16[8,3584]{1,0:T(8,128)(2,1)S(1)}, bf16[8,3584]{1,0:T(8,128)(2,1)S(1)}, u32[]{:S(2)}, u32[]{:S(2)}) collective-permute-start(bf16[8,3584]{1,0:T(8,128)(2,1)S(1)} %slice.196), channel_id=1, source_target_pairs={{0,4},{1,5},{4,8},{5,9},{8,12},{9,13},{12,14},{13,15},{14,10},{15,... | collective-permute-start | bytes 172040 | tf_op jit(solution)/shard_map/ppermute | solution.py:106
  22.1 1.6 %collective-permute-start.10 = (bf16[8,7168]{1,0:T(8,128)(2,1)S(1)}, bf16[8,7168]{1,0:T(8,128)(2,1)S(1)}, u32[]{:S(2)}, u32[]{:S(2)}) collective-permute-start(bf16[8,7168]{1,0:T(8,128)(2,1)S(1)} %collective-permute-done.9), channel_id=1, source_target_pairs={{0,1},{1,0},{2,3},{3,2},{4,5},{5,4},{6,7},{7,6},{8,9},{9,8},{10,11... | collective-permute-start | bytes 344072 | tf_op jit(solution)/shard_map/ppermute | solution.py:106
  23.8 2.0 %collective-permute-start.16 = (bf16[8,3584]{1,0:T(8,128)(2,1)S(1)}, bf16[8,3584]{1,0:T(8,128)(2,1)S(1)}, u32[]{:S(2)}, u32[]{:S(2)}) collective-permute-start(bf16[8,3584]{1,0:T(8,128)(2,1)S(1)} %collective-permute-done.14), channel_id=1, source_target_pairs={{0,1},{1,0},{2,3},{3,2},{4,5},{5,4},{6,7},{7,6},{8,9},{9,8},{10,11... | collective-permute-start | bytes 172040 | tf_op jit(solution)/shard_map/ppermute | solution.py:106
  27.1 0.7 fusion.4
  27.8 0.8 copy-done.3
  28.6 0.7 fusion.6
  29.3 0.8 copy-done.2
  30.1 0.6 convolution_convert_fusion.2
  31.4 0.8 collective-permute-done.20
  32.6 1.5 %collective-permute-start.22 = (bf16[8,3584]{1,0:T(8,128)(2,1)S(1)}, bf16[8,3584]{1,0:T(8,128)(2,1)S(1)}, u32[]{:S(2)}, u32[]{:S(2)}) collective-permute-start(bf16[8,3584]{1,0:T(8,128)(2,1)S(1)} %get-tuple-element.35), channel_id=1, source_target_pairs={{0,4},{1,5},{4,8},{5,9},{8,12},{9,13},{12,14},{13,15},{14,10},{15,... | collective-permute-start | bytes 172040 | tf_op jit(solution)/shard_map/ppermute | solution.py:106
  34.6 1.1 collective-permute-done.22
  35.7 1.5 %collective-permute-start.23 = (bf16[8,7168]{1,0:T(8,128)(2,1)S(1)}, bf16[8,7168]{1,0:T(8,128)(2,1)S(1)}, u32[]{:S(2)}, u32[]{:S(2)}) collective-permute-start(bf16[8,7168]{1,0:T(8,128)(2,1)S(1)} %pad_maximum_fusion), channel_id=1, source_target_pairs={{0,4},{1,5},{4,8},{5,9},{8,12},{9,13},{12,14},{13,15},{14,10},{15,... | collective-permute-start | bytes 344072 | tf_op jit(solution)/shard_map/ppermute | solution.py:106
  37.3 1.6 %collective-permute-start.18 = (bf16[8,7168]{1,0:T(8,128)(2,1)S(1)}, bf16[8,7168]{1,0:T(8,128)(2,1)S(1)}, u32[]{:S(2)}, u32[]{:S(2)}) collective-permute-start(bf16[8,7168]{1,0:T(8,128)(2,1)S(1)} %get-tuple-element.28), channel_id=1, source_target_pairs={{0,1},{1,0},{2,3},{3,2},{4,5},{5,4},{6,7},{7,6},{8,9},{9,8},{10,11... | collective-permute-start | bytes 344072 | tf_op jit(solution)/shard_map/ppermute | solution.py:106
  38.9 0.6 collective-permute-done.23
  39.5 1.5 %collective-permute-start.24 = (bf16[8,7168]{1,0:T(8,128)(2,1)S(1)}, bf16[8,7168]{1,0:T(8,128)(2,1)S(1)}, u32[]{:S(2)}, u32[]{:S(2)}) collective-permute-start(bf16[8,7168]{1,0:T(8,128)(2,1)S(1)} %fusion.26), channel_id=1, source_target_pairs={{0,4},{1,5},{4,8},{5,9},{8,12},{9,13},{12,14},{13,15},{14,10},{15,... | collective-permute-start | bytes 344072 | tf_op jit(solution)/shard_map/ppermute | solution.py:106
  41.0 2.7 %collective-permute-start.27 = (bf16[8,7168]{1,0:T(8,128)(2,1)S(1)}, bf16[8,7168]{1,0:T(8,128)(2,1)S(1)}, u32[]{:S(2)}, u32[]{:S(2)}) collective-permute-start(bf16[8,7168]{1,0:T(8,128)(2,1)S(1)} %get-tuple-element.23), channel_id=1, source_target_pairs={{0,1},{1,0},{2,3},{3,2},{4,5},{5,4},{6,7},{7,6},{8,9},{9,8},{10,11... | collective-permute-start | bytes 344072 | tf_op jit(solution)/shard_map/ppermute | solution.py:106
  43.9 3.4 %collective-permute-done.29 = bf16[8,3584]{1,0:T(8,128)(2,1)S(1)} collective-permute-done((bf16[8,3584]{1,0:T(8,128)(2,1)S(1)}, bf16[8,3584]{1,0:T(8,128)(2,1)S(1)}, u32[]{:S(2)}, u32[]{:S(2)}) %collective-permute-start.29) | collective-permute-done | bytes 57376 | tf_op jit(solution)/shard_map/ppermute | solution.py:106
  47.4 1.3 %collective-permute-start.26 = (bf16[8,7168]{1,0:T(8,128)(2,1)S(1)}, bf16[8,7168]{1,0:T(8,128)(2,1)S(1)}, u32[]{:S(2)}, u32[]{:S(2)}) collective-permute-start(bf16[8,7168]{1,0:T(8,128)(2,1)S(1)} %get-tuple-element.24), channel_id=1, source_target_pairs={{0,1},{1,0},{2,3},{3,2},{4,5},{5,4},{6,7},{7,6},{8,9},{9,8},{10,11... | collective-permute-start | bytes 344072 | tf_op jit(solution)/shard_map/ppermute | solution.py:106
  48.7 2.4 %collective-permute-done.30 = bf16[8,7168]{1,0:T(8,128)(2,1)S(1)} collective-permute-done((bf16[8,7168]{1,0:T(8,128)(2,1)S(1)}, bf16[8,7168]{1,0:T(8,128)(2,1)S(1)}, u32[]{:S(2)}, u32[]{:S(2)}) %collective-permute-start.30) | collective-permute-done | bytes 114720 | tf_op jit(solution)/shard_map/ppermute | solution.py:106
  51.2 2.4 %collective-permute-start.17 = (bf16[8,7168]{1,0:T(8,128)(2,1)S(1)}, bf16[8,7168]{1,0:T(8,128)(2,1)S(1)}, u32[]{:S(2)}, u32[]{:S(2)}) collective-permute-start(bf16[8,7168]{1,0:T(8,128)(2,1)S(1)} %get-tuple-element.21), channel_id=1, source_target_pairs={{0,1},{1,0},{2,3},{3,2},{4,5},{5,4},{6,7},{7,6},{8,9},{9,8},{10,11... | collective-permute-start | bytes 344072 | tf_op jit(solution)/shard_map/ppermute | solution.py:106
  53.6 1.3 %collective-permute-start.25 = (bf16[8,7168]{1,0:T(8,128)(2,1)S(1)}, bf16[8,7168]{1,0:T(8,128)(2,1)S(1)}, u32[]{:S(2)}, u32[]{:S(2)}) collective-permute-start(bf16[8,7168]{1,0:T(8,128)(2,1)S(1)} %get-tuple-element.29), channel_id=1, source_target_pairs={{0,4},{1,5},{4,8},{5,9},{8,12},{9,13},{12,14},{13,15},{14,10},{15,... | collective-permute-start | bytes 344072 | tf_op jit(solution)/shard_map/ppermute | solution.py:106
  55.3 3.1 %collective-permute-done.25 = bf16[8,7168]{1,0:T(8,128)(2,1)S(1)} collective-permute-done((bf16[8,7168]{1,0:T(8,128)(2,1)S(1)}, bf16[8,7168]{1,0:T(8,128)(2,1)S(1)}, u32[]{:S(2)}, u32[]{:S(2)}) %collective-permute-start.25) | collective-permute-done | bytes 114720 | tf_op jit(solution)/shard_map/ppermute | solution.py:106
  59.3 1.3 %collective-permute-start.34 = (bf16[8,7168]{1,0:T(8,128)(2,1)S(1)}, bf16[8,7168]{1,0:T(8,128)(2,1)S(1)}, u32[]{:S(2)}, u32[]{:S(2)}) collective-permute-start(bf16[8,7168]{1,0:T(8,128)(2,1)S(1)} %get-tuple-element.6), channel_id=1, source_target_pairs={{0,4},{1,5},{4,8},{5,9},{8,12},{9,13},{12,14},{13,15},{14,10},{15,... | collective-permute-start | bytes 344072 | tf_op jit(solution)/shard_map/ppermute | solution.py:106
  60.8 4.6 %collective-permute-start.33 = (bf16[8,7168]{1,0:T(8,128)(2,1)S(1)}, bf16[8,7168]{1,0:T(8,128)(2,1)S(1)}, u32[]{:S(2)}, u32[]{:S(2)}) collective-permute-start(bf16[8,7168]{1,0:T(8,128)(2,1)S(1)} %get-tuple-element.6), channel_id=1, source_target_pairs={{0,1},{1,0},{2,3},{3,2},{4,5},{5,4},{6,7},{7,6},{8,9},{9,8},{10,11... | collective-permute-start | bytes 344072 | tf_op jit(solution)/shard_map/ppermute | solution.py:106
  65.4 2.8 %collective-permute-start.35 = (bf16[8,7168]{1,0:T(8,128)(2,1)S(1)}, bf16[8,7168]{1,0:T(8,128)(2,1)S(1)}, u32[]{:S(2)}, u32[]{:S(2)}) collective-permute-start(bf16[8,7168]{1,0:T(8,128)(2,1)S(1)} %collective-permute-done.34), channel_id=1, source_target_pairs={{0,1},{1,0},{2,3},{3,2},{4,5},{5,4},{6,7},{7,6},{8,9},{9,8},{10,11... | collective-permute-start | bytes 344072 | tf_op jit(solution)/shard_map/ppermute | solution.py:106
  68.2 1.3 %collective-permute-start.38 = (bf16[8,7168]{1,0:T(8,128)(2,1)S(1)}, bf16[8,7168]{1,0:T(8,128)(2,1)S(1)}, u32[]{:S(2)}, u32[]{:S(2)}) collective-permute-start(bf16[8,7168]{1,0:T(8,128)(2,1)S(1)} %collective-permute-done.34), channel_id=1, source_target_pairs={{0,4},{1,5},{4,8},{5,9},{8,12},{9,13},{12,14},{13,15},{14,10},{15,... | collective-permute-start | bytes 344072 | tf_op jit(solution)/shard_map/ppermute | solution.py:106
  70.0 3.0 %collective-permute-done.38 = bf16[8,7168]{1,0:T(8,128)(2,1)S(1)} collective-permute-done((bf16[8,7168]{1,0:T(8,128)(2,1)S(1)}, bf16[8,7168]{1,0:T(8,128)(2,1)S(1)}, u32[]{:S(2)}, u32[]{:S(2)}) %collective-permute-start.38) | collective-permute-done | bytes 114720 | tf_op jit(solution)/shard_map/ppermute | solution.py:106
  73.0 0.8 collective-permute-start.39
  73.7 1.3 %collective-permute-start.42 = (bf16[8,7168]{1,0:T(8,128)(2,1)S(1)}, bf16[8,7168]{1,0:T(8,128)(2,1)S(1)}, u32[]{:S(2)}, u32[]{:S(2)}) collective-permute-start(bf16[8,7168]{1,0:T(8,128)(2,1)S(1)} %collective-permute-done.38), channel_id=1, source_target_pairs={{0,4},{1,5},{4,8},{5,9},{8,12},{9,13},{12,14},{13,15},{14,10},{15,... | collective-permute-start | bytes 344072 | tf_op jit(solution)/shard_map/ppermute | solution.py:106
  75.6 4.3 %collective-permute-done.44 = bf16[8,7168]{1,0:T(8,128)(2,1)S(1)} collective-permute-done((bf16[8,7168]{1,0:T(8,128)(2,1)S(1)}, bf16[8,7168]{1,0:T(8,128)(2,1)S(1)}, u32[]{:S(2)}, u32[]{:S(2)}) %collective-permute-start.44) | collective-permute-done | bytes 114720 | tf_op jit(solution)/shard_map/ppermute | solution.py:106
  80.0 1.4 %collective-permute-start.46 = (bf16[8,3584]{1,0:T(8,128)(2,1)S(1)}, bf16[8,3584]{1,0:T(8,128)(2,1)S(1)}, u32[]{:S(2)}, u32[]{:S(2)}) collective-permute-start(bf16[8,3584]{1,0:T(8,128)(2,1)S(1)} %slice.220), channel_id=1, source_target_pairs={{0,4},{1,5},{4,8},{5,9},{8,12},{9,13},{12,14},{13,15},{14,10},{15,... | collective-permute-start | bytes 172040 | tf_op jit(solution)/shard_map/ppermute | solution.py:106
  81.4 1.6 %collective-permute-start.43 = (bf16[8,7168]{1,0:T(8,128)(2,1)S(1)}, bf16[8,7168]{1,0:T(8,128)(2,1)S(1)}, u32[]{:S(2)}, u32[]{:S(2)}) collective-permute-start(bf16[8,7168]{1,0:T(8,128)(2,1)S(1)} %collective-permute-done.42), channel_id=1, source_target_pairs={{0,1},{1,0},{2,3},{3,2},{4,5},{5,4},{6,7},{7,6},{8,9},{9,8},{10,11... | collective-permute-start | bytes 344072 | tf_op jit(solution)/shard_map/ppermute | solution.py:106
  83.1 2.0 %collective-permute-start.49 = (bf16[8,3584]{1,0:T(8,128)(2,1)S(1)}, bf16[8,3584]{1,0:T(8,128)(2,1)S(1)}, u32[]{:S(2)}, u32[]{:S(2)}) collective-permute-start(bf16[8,3584]{1,0:T(8,128)(2,1)S(1)} %collective-permute-done.47), channel_id=1, source_target_pairs={{0,1},{1,0},{2,3},{3,2},{4,5},{5,4},{6,7},{7,6},{8,9},{9,8},{10,11... | collective-permute-start | bytes 172040 | tf_op jit(solution)/shard_map/ppermute | solution.py:106
  86.0 0.5 collective-permute-done.48
  86.5 0.6 fusion.2
  87.1 0.6 fusion.43
  87.8 0.6 fusion
  89.1 0.8 collective-permute-done.53
  90.3 1.4 %collective-permute-start.55 = (bf16[8,3584]{1,0:T(8,128)(2,1)S(1)}, bf16[8,3584]{1,0:T(8,128)(2,1)S(1)}, u32[]{:S(2)}, u32[]{:S(2)}) collective-permute-start(bf16[8,3584]{1,0:T(8,128)(2,1)S(1)} %get-tuple-element.33), channel_id=1, source_target_pairs={{0,4},{1,5},{4,8},{5,9},{8,12},{9,13},{12,14},{13,15},{14,10},{15,... | collective-permute-start | bytes 172040 | tf_op jit(solution)/shard_map/ppermute | solution.py:106
  92.1 1.3 %collective-permute-done.55 = bf16[8,3584]{1,0:T(8,128)(2,1)S(1)} collective-permute-done((bf16[8,3584]{1,0:T(8,128)(2,1)S(1)}, bf16[8,3584]{1,0:T(8,128)(2,1)S(1)}, u32[]{:S(2)}, u32[]{:S(2)}) %collective-permute-start.55) | collective-permute-done | bytes 57376 | tf_op jit(solution)/shard_map/ppermute | solution.py:106
  93.4 1.4 %collective-permute-start.56 = (bf16[8,7168]{1,0:T(8,128)(2,1)S(1)}, bf16[8,7168]{1,0:T(8,128)(2,1)S(1)}, u32[]{:S(2)}, u32[]{:S(2)}) collective-permute-start(bf16[8,7168]{1,0:T(8,128)(2,1)S(1)} %pad_maximum_fusion.2), channel_id=1, source_target_pairs={{0,4},{1,5},{4,8},{5,9},{8,12},{9,13},{12,14},{13,15},{14,10},{15,... | collective-permute-start | bytes 344072 | tf_op jit(solution)/shard_map/ppermute | solution.py:106
  94.8 1.6 %collective-permute-start.51 = (bf16[8,7168]{1,0:T(8,128)(2,1)S(1)}, bf16[8,7168]{1,0:T(8,128)(2,1)S(1)}, u32[]{:S(2)}, u32[]{:S(2)}) collective-permute-start(bf16[8,7168]{1,0:T(8,128)(2,1)S(1)} %get-tuple-element.16), channel_id=1, source_target_pairs={{0,1},{1,0},{2,3},{3,2},{4,5},{5,4},{6,7},{7,6},{8,9},{9,8},{10,11... | collective-permute-start | bytes 344072 | tf_op jit(solution)/shard_map/ppermute | solution.py:106
  96.4 0.7 collective-permute-done.56
  97.2 1.4 %collective-permute-start.57 = (bf16[8,7168]{1,0:T(8,128)(2,1)S(1)}, bf16[8,7168]{1,0:T(8,128)(2,1)S(1)}, u32[]{:S(2)}, u32[]{:S(2)}) collective-permute-start(bf16[8,7168]{1,0:T(8,128)(2,1)S(1)} %fusion.14), channel_id=1, source_target_pairs={{0,4},{1,5},{4,8},{5,9},{8,12},{9,13},{12,14},{13,15},{14,10},{15,... | collective-permute-start | bytes 344072 | tf_op jit(solution)/shard_map/ppermute | solution.py:106
  98.5 2.7 %collective-permute-start.60 = (bf16[8,7168]{1,0:T(8,128)(2,1)S(1)}, bf16[8,7168]{1,0:T(8,128)(2,1)S(1)}, u32[]{:S(2)}, u32[]{:S(2)}) collective-permute-start(bf16[8,7168]{1,0:T(8,128)(2,1)S(1)} %get-tuple-element.11), channel_id=1, source_target_pairs={{0,1},{1,0},{2,3},{3,2},{4,5},{5,4},{6,7},{7,6},{8,9},{9,8},{10,11... | collective-permute-start | bytes 344072 | tf_op jit(solution)/shard_map/ppermute | solution.py:106
  101.5 3.3 %collective-permute-done.62 = bf16[8,3584]{1,0:T(8,128)(2,1)S(1)} collective-permute-done((bf16[8,3584]{1,0:T(8,128)(2,1)S(1)}, bf16[8,3584]{1,0:T(8,128)(2,1)S(1)}, u32[]{:S(2)}, u32[]{:S(2)}) %collective-permute-start.62) | collective-permute-done | bytes 57376 | tf_op jit(solution)/shard_map/ppermute | solution.py:106
  105.2 1.1 collective-permute-start.59
  106.3 2.2 %collective-permute-done.63 = bf16[8,7168]{1,0:T(8,128)(2,1)S(1)} collective-permute-done((bf16[8,7168]{1,0:T(8,128)(2,1)S(1)}, bf16[8,7168]{1,0:T(8,128)(2,1)S(1)}, u32[]{:S(2)}, u32[]{:S(2)}) %collective-permute-start.63) | collective-permute-done | bytes 114720 | tf_op jit(solution)/shard_map/ppermute | solution.py:106
  108.8 1.9 %convolution_convert_fusion.1 = bf16[128,7168]{1,0:T(8,128)(2,1)} fusion(f32[8]{0:T(128)S(1)} %get-tuple-element.4, bf16[8,7168]{1,0:T(8,128)(2,1)S(1)} %collective-permute-done.32, bf16[8,7168]{1,0:T(8,128)(2,1)S(1)} %collective-permute-done.25, bf16[8,7168]{1,0:T(8,128)(2,1)S(1)} %collective-permute-done.17, bf16[8,2,8,7168]{3,2,1,0:T(8,128)(2,1)S(1)} %bitcast.217, ...), kind=kOutput, calls=%fused_computation.3 | convolution fusion | flops 16117760 | bytes 2295296 | tf_op jit(solution)/shard_map/st,sd->td/dot_general | solution.py:161
  110.7 2.2 %collective-permute-start.50 = (bf16[8,7168]{1,0:T(8,128)(2,1)S(1)}, bf16[8,7168]{1,0:T(8,128)(2,1)S(1)}, u32[]{:S(2)}, u32[]{:S(2)}) collective-permute-start(bf16[8,7168]{1,0:T(8,128)(2,1)S(1)} %get-tuple-element.9), channel_id=1, source_target_pairs={{0,1},{1,0},{2,3},{3,2},{4,5},{5,4},{6,7},{7,6},{8,9},{9,8},{10,11... | collective-permute-start | bytes 344072 | tf_op jit(solution)/shard_map/ppermute | solution.py:106
  113.0 1.3 %collective-permute-start.58 = (bf16[8,7168]{1,0:T(8,128)(2,1)S(1)}, bf16[8,7168]{1,0:T(8,128)(2,1)S(1)}, u32[]{:S(2)}, u32[]{:S(2)}) collective-permute-start(bf16[8,7168]{1,0:T(8,128)(2,1)S(1)} %get-tuple-element.17), channel_id=1, source_target_pairs={{0,4},{1,5},{4,8},{5,9},{8,12},{9,13},{12,14},{13,15},{14,10},{15,... | collective-permute-start | bytes 344072 | tf_op jit(solution)/shard_map/ppermute | solution.py:106
  114.5 0.6 broadcast_select_fusion
  115.1 2.6 %collective-permute-done.58 = bf16[8,7168]{1,0:T(8,128)(2,1)S(1)} collective-permute-done((bf16[8,7168]{1,0:T(8,128)(2,1)S(1)}, bf16[8,7168]{1,0:T(8,128)(2,1)S(1)}, u32[]{:S(2)}, u32[]{:S(2)}) %collective-permute-start.58) | collective-permute-done | bytes 114720 | tf_op jit(solution)/shard_map/ppermute | solution.py:106
  118.1 1.9 %convolution_convert_fusion = bf16[128,7168]{1,0:T(8,128)(2,1)} fusion(bf16[8,7168]{1,0:T(8,128)(2,1)S(1)} %collective-permute-done.65, bf16[8,7168]{1,0:T(8,128)(2,1)S(1)} %collective-permute-done.58, bf16[8,7168]{1,0:T(8,128)(2,1)S(1)} %collective-permute-done.50, bf16[8,2,8,7168]{3,2,1,0:T(8,128)(2,1)S(1)} %bitcast.224, s32[128]{0:T(128)S(1)} %add_reduce_fusion, ...), kind=kOutput, calls=%fused_computation.2 | convolution fusion | flops 16060416 | bytes 2294784 | tf_op jit(solution)/shard_map/st,sd->td/dot_general | solution.py:162
  (158 shorter events, 11.7 us)
Async XLA Ops:
  2.5 5.0 %collective-permute-start.1 = (bf16[8,7168]{1,0:T(8,128)(2,1)S(1)}, bf16[8,7168]{1,0:T(8,128)(2,1)S(1)}, u32[]{:S(2)}, u32[]{:S(2)}) collective-permute-start(bf16[8,7168]{1,0:T(8,128)(2,1)S(1)} %get-tuple-element.38), channel_id=1, source_target_pairs={{0,4},{1,5},{4,8},{5,9},{8,12},{9,13},{12,14},{13,15},{14,10},{15,... | collective-permute-start | bytes 344072 | tf_op jit(solution)/shard_map/ppermute | solution.py:106
  4.7 5.6 %collective-permute-start.3 = (bf16[8,7168]{1,0:T(8,128)(2,1)S(1)}, bf16[8,7168]{1,0:T(8,128)(2,1)S(1)}, u32[]{:S(2)}, u32[]{:S(2)}) collective-permute-start(bf16[8,7168]{1,0:T(8,128)(2,1)S(1)} %get-tuple-element.38), channel_id=1, source_target_pairs={{0,2},{1,3},{4,0},{5,1},{8,4},{9,5},{12,8},{13,9},{14,12},{15,13},... | collective-permute-start | bytes 344072 | tf_op jit(solution)/shard_map/ppermute | solution.py:106
  4.7 5.8 %collective-permute-start = (bf16[8,7168]{1,0:T(8,128)(2,1)S(1)}, bf16[8,7168]{1,0:T(8,128)(2,1)S(1)}, u32[]{:S(2)}, u32[]{:S(2)}) collective-permute-start(bf16[8,7168]{1,0:T(8,128)(2,1)S(1)} %get-tuple-element.38), channel_id=1, source_target_pairs={{0,1},{1,0},{2,3},{3,2},{4,5},{5,4},{6,7},{7,6},{8,9},{9,8},{10,11... | collective-permute-start | bytes 344072 | tf_op jit(solution)/shard_map/ppermute | solution.py:106
  7.5 8.6 %collective-permute-start.2 = (bf16[8,7168]{1,0:T(8,128)(2,1)S(1)}, bf16[8,7168]{1,0:T(8,128)(2,1)S(1)}, u32[]{:S(2)}, u32[]{:S(2)}) collective-permute-start(bf16[8,7168]{1,0:T(8,128)(2,1)S(1)} %collective-permute-done.1), channel_id=1, source_target_pairs={{0,1},{1,0},{2,3},{3,2},{4,5},{5,4},{6,7},{7,6},{8,9},{9,8},{10,11... | collective-permute-start | bytes 344072 | tf_op jit(solution)/shard_map/ppermute | solution.py:106
  8.7 4.8 %collective-permute-start.5 = (bf16[8,7168]{1,0:T(8,128)(2,1)S(1)}, bf16[8,7168]{1,0:T(8,128)(2,1)S(1)}, u32[]{:S(2)}, u32[]{:S(2)}) collective-permute-start(bf16[8,7168]{1,0:T(8,128)(2,1)S(1)} %collective-permute-done.1), channel_id=1, source_target_pairs={{0,4},{1,5},{4,8},{5,9},{8,12},{9,13},{12,14},{13,15},{14,10},{15,... | collective-permute-start | bytes 344072 | tf_op jit(solution)/shard_map/ppermute | solution.py:106
  10.2 5.9 %collective-permute-start.4 = (bf16[8,7168]{1,0:T(8,128)(2,1)S(1)}, bf16[8,7168]{1,0:T(8,128)(2,1)S(1)}, u32[]{:S(2)}, u32[]{:S(2)}) collective-permute-start(bf16[8,7168]{1,0:T(8,128)(2,1)S(1)} %collective-permute-done.3), channel_id=1, source_target_pairs={{0,1},{1,0},{2,3},{3,2},{4,5},{5,4},{6,7},{7,6},{8,9},{9,8},{10,11... | collective-permute-start | bytes 344072 | tf_op jit(solution)/shard_map/ppermute | solution.py:106
  10.5 5.3 %collective-permute-start.7 = (bf16[8,7168]{1,0:T(8,128)(2,1)S(1)}, bf16[8,7168]{1,0:T(8,128)(2,1)S(1)}, u32[]{:S(2)}, u32[]{:S(2)}) collective-permute-start(bf16[8,7168]{1,0:T(8,128)(2,1)S(1)} %collective-permute-done.3), channel_id=1, source_target_pairs={{0,2},{1,3},{4,0},{5,1},{8,4},{9,5},{12,8},{13,9},{14,12},{15,13},... | collective-permute-start | bytes 344072 | tf_op jit(solution)/shard_map/ppermute | solution.py:106
  13.5 10.3 %collective-permute-start.6 = (bf16[8,7168]{1,0:T(8,128)(2,1)S(1)}, bf16[8,7168]{1,0:T(8,128)(2,1)S(1)}, u32[]{:S(2)}, u32[]{:S(2)}) collective-permute-start(bf16[8,7168]{1,0:T(8,128)(2,1)S(1)} %collective-permute-done.5), channel_id=1, source_target_pairs={{0,1},{1,0},{2,3},{3,2},{4,5},{5,4},{6,7},{7,6},{8,9},{9,8},{10,11... | collective-permute-start | bytes 344072 | tf_op jit(solution)/shard_map/ppermute | solution.py:106
  14.3 6.4 %collective-permute-start.9 = (bf16[8,7168]{1,0:T(8,128)(2,1)S(1)}, bf16[8,7168]{1,0:T(8,128)(2,1)S(1)}, u32[]{:S(2)}, u32[]{:S(2)}) collective-permute-start(bf16[8,7168]{1,0:T(8,128)(2,1)S(1)} %collective-permute-done.5), channel_id=1, source_target_pairs={{0,4},{1,5},{4,8},{5,9},{8,12},{9,13},{12,14},{13,15},{14,10},{15,... | collective-permute-start | bytes 344072 | tf_op jit(solution)/shard_map/ppermute | solution.py:106
  15.8 8.0 %collective-permute-start.8 = (bf16[8,7168]{1,0:T(8,128)(2,1)S(1)}, bf16[8,7168]{1,0:T(8,128)(2,1)S(1)}, u32[]{:S(2)}, u32[]{:S(2)}) collective-permute-start(bf16[8,7168]{1,0:T(8,128)(2,1)S(1)} %collective-permute-done.7), channel_id=1, source_target_pairs={{0,1},{1,0},{2,3},{3,2},{4,5},{5,4},{6,7},{7,6},{8,9},{9,8},{10,11... | collective-permute-start | bytes 344072 | tf_op jit(solution)/shard_map/ppermute | solution.py:106
  16.1 4.5 %collective-permute-start.11 = (bf16[8,7168]{1,0:T(8,128)(2,1)S(1)}, bf16[8,7168]{1,0:T(8,128)(2,1)S(1)}, u32[]{:S(2)}, u32[]{:S(2)}) collective-permute-start(bf16[8,7168]{1,0:T(8,128)(2,1)S(1)} %collective-permute-done.7), channel_id=1, source_target_pairs={{0,2},{1,3},{4,0},{5,1},{8,4},{9,5},{12,8},{13,9},{14,12},{15,13},... | collective-permute-start | bytes 344072 | tf_op jit(solution)/shard_map/ppermute | solution.py:106
  20.6 3.2 %collective-permute-start.14 = (bf16[8,3584]{1,0:T(8,128)(2,1)S(1)}, bf16[8,3584]{1,0:T(8,128)(2,1)S(1)}, u32[]{:S(2)}, u32[]{:S(2)}) collective-permute-start(bf16[8,3584]{1,0:T(8,128)(2,1)S(1)} %slice.197), channel_id=1, source_target_pairs={{0,2},{1,3},{4,0},{5,1},{8,4},{9,5},{12,8},{13,9},{14,12},{15,13},... | collective-permute-start | bytes 172040 | tf_op jit(solution)/shard_map/ppermute | solution.py:106
  20.7 5.1 %collective-permute-start.13 = (bf16[8,3584]{1,0:T(8,128)(2,1)S(1)}, bf16[8,3584]{1,0:T(8,128)(2,1)S(1)}, u32[]{:S(2)}, u32[]{:S(2)}) collective-permute-start(bf16[8,3584]{1,0:T(8,128)(2,1)S(1)} %slice.196), channel_id=1, source_target_pairs={{0,4},{1,5},{4,8},{5,9},{8,12},{9,13},{12,14},{13,15},{14,10},{15,... | collective-permute-start | bytes 172040 | tf_op jit(solution)/shard_map/ppermute | solution.py:106
  22.1 4.0 %collective-permute-start.10 = (bf16[8,7168]{1,0:T(8,128)(2,1)S(1)}, bf16[8,7168]{1,0:T(8,128)(2,1)S(1)}, u32[]{:S(2)}, u32[]{:S(2)}) collective-permute-start(bf16[8,7168]{1,0:T(8,128)(2,1)S(1)} %collective-permute-done.9), channel_id=1, source_target_pairs={{0,1},{1,0},{2,3},{3,2},{4,5},{5,4},{6,7},{7,6},{8,9},{9,8},{10,11... | collective-permute-start | bytes 344072 | tf_op jit(solution)/shard_map/ppermute | solution.py:106
  23.7 2.5 %collective-permute-start.12 = (bf16[8,7168]{1,0:T(8,128)(2,1)S(1)}, bf16[8,7168]{1,0:T(8,128)(2,1)S(1)}, u32[]{:S(2)}, u32[]{:S(2)}) collective-permute-start(bf16[8,7168]{1,0:T(8,128)(2,1)S(1)} %collective-permute-done.11), channel_id=1, source_target_pairs={{0,1},{1,0},{2,3},{3,2},{4,5},{5,4},{6,7},{7,6},{8,9},{9,8},{10,11... | collective-permute-start | bytes 344072 | tf_op jit(solution)/shard_map/ppermute | solution.py:106
  23.8 2.9 %collective-permute-start.16 = (bf16[8,3584]{1,0:T(8,128)(2,1)S(1)}, bf16[8,3584]{1,0:T(8,128)(2,1)S(1)}, u32[]{:S(2)}, u32[]{:S(2)}) collective-permute-start(bf16[8,3584]{1,0:T(8,128)(2,1)S(1)} %collective-permute-done.14), channel_id=1, source_target_pairs={{0,1},{1,0},{2,3},{3,2},{4,5},{5,4},{6,7},{7,6},{8,9},{9,8},{10,11... | collective-permute-start | bytes 172040 | tf_op jit(solution)/shard_map/ppermute | solution.py:106
  30.8 1.4 %collective-permute-start.20 = (bf16[8,7168]{1,0:T(8,128)(2,1)S(1)}, bf16[8,7168]{1,0:T(8,128)(2,1)S(1)}, u32[]{:S(2)}, u32[]{:S(2)}) collective-permute-start(bf16[8,7168]{1,0:T(8,128)(2,1)S(1)} %get-tuple-element.26), channel_id=1, source_target_pairs={{0,1},{1,0},{2,3},{3,2},{4,5},{5,4},{6,7},{7,6},{8,9},{9,8},{10,11... | collective-permute-start | bytes 344072 | tf_op jit(solution)/shard_map/ppermute | solution.py:106
  31.2 1.3 %collective-permute-start.21 = (bf16[8,7168]{1,0:T(8,128)(2,1)S(1)}, bf16[8,7168]{1,0:T(8,128)(2,1)S(1)}, u32[]{:S(2)}, u32[]{:S(2)}) collective-permute-start(bf16[8,7168]{1,0:T(8,128)(2,1)S(1)} %get-tuple-element.25), channel_id=1, source_target_pairs={{0,1},{1,0},{2,3},{3,2},{4,5},{5,4},{6,7},{7,6},{8,9},{9,8},{10,11... | collective-permute-start | bytes 344072 | tf_op jit(solution)/shard_map/ppermute | solution.py:106
  32.6 3.1 %collective-permute-start.22 = (bf16[8,3584]{1,0:T(8,128)(2,1)S(1)}, bf16[8,3584]{1,0:T(8,128)(2,1)S(1)}, u32[]{:S(2)}, u32[]{:S(2)}) collective-permute-start(bf16[8,3584]{1,0:T(8,128)(2,1)S(1)} %get-tuple-element.35), channel_id=1, source_target_pairs={{0,4},{1,5},{4,8},{5,9},{8,12},{9,13},{12,14},{13,15},{14,10},{15,... | collective-permute-start | bytes 172040 | tf_op jit(solution)/shard_map/ppermute | solution.py:106
  34.2 4.7 %collective-permute-start.19 = (bf16[8,7168]{1,0:T(8,128)(2,1)S(1)}, bf16[8,7168]{1,0:T(8,128)(2,1)S(1)}, u32[]{:S(2)}, u32[]{:S(2)}) collective-permute-start(bf16[8,7168]{1,0:T(8,128)(2,1)S(1)} %get-tuple-element.27), channel_id=1, source_target_pairs={{0,1},{1,0},{2,3},{3,2},{4,5},{5,4},{6,7},{7,6},{8,9},{9,8},{10,11... | collective-permute-start | bytes 344072 | tf_op jit(solution)/shard_map/ppermute | solution.py:106
  35.7 3.7 %collective-permute-start.23 = (bf16[8,7168]{1,0:T(8,128)(2,1)S(1)}, bf16[8,7168]{1,0:T(8,128)(2,1)S(1)}, u32[]{:S(2)}, u32[]{:S(2)}) collective-permute-start(bf16[8,7168]{1,0:T(8,128)(2,1)S(1)} %pad_maximum_fusion), channel_id=1, source_target_pairs={{0,4},{1,5},{4,8},{5,9},{8,12},{9,13},{12,14},{13,15},{14,10},{15,... | collective-permute-start | bytes 344072 | tf_op jit(solution)/shard_map/ppermute | solution.py:106
  37.3 6.5 %collective-permute-start.18 = (bf16[8,7168]{1,0:T(8,128)(2,1)S(1)}, bf16[8,7168]{1,0:T(8,128)(2,1)S(1)}, u32[]{:S(2)}, u32[]{:S(2)}) collective-permute-start(bf16[8,7168]{1,0:T(8,128)(2,1)S(1)} %get-tuple-element.28), channel_id=1, source_target_pairs={{0,1},{1,0},{2,3},{3,2},{4,5},{5,4},{6,7},{7,6},{8,9},{9,8},{10,11... | collective-permute-start | bytes 344072 | tf_op jit(solution)/shard_map/ppermute | solution.py:106
  38.9 4.9 %collective-permute-start.28 = (bf16[8,7168]{1,0:T(8,128)(2,1)S(1)}, bf16[8,7168]{1,0:T(8,128)(2,1)S(1)}, u32[]{:S(2)}, u32[]{:S(2)}) collective-permute-start(bf16[8,7168]{1,0:T(8,128)(2,1)S(1)} %get-tuple-element.22), channel_id=1, source_target_pairs={{0,1},{1,0},{2,3},{3,2},{4,5},{5,4},{6,7},{7,6},{8,9},{9,8},{10,11... | collective-permute-start | bytes 344072 | tf_op jit(solution)/shard_map/ppermute | solution.py:106
  39.5 4.3 %collective-permute-start.24 = (bf16[8,7168]{1,0:T(8,128)(2,1)S(1)}, bf16[8,7168]{1,0:T(8,128)(2,1)S(1)}, u32[]{:S(2)}, u32[]{:S(2)}) collective-permute-start(bf16[8,7168]{1,0:T(8,128)(2,1)S(1)} %fusion.26), channel_id=1, source_target_pairs={{0,4},{1,5},{4,8},{5,9},{8,12},{9,13},{12,14},{13,15},{14,10},{15,... | collective-permute-start | bytes 344072 | tf_op jit(solution)/shard_map/ppermute | solution.py:106
  41.0 7.7 %collective-permute-start.27 = (bf16[8,7168]{1,0:T(8,128)(2,1)S(1)}, bf16[8,7168]{1,0:T(8,128)(2,1)S(1)}, u32[]{:S(2)}, u32[]{:S(2)}) collective-permute-start(bf16[8,7168]{1,0:T(8,128)(2,1)S(1)} %get-tuple-element.23), channel_id=1, source_target_pairs={{0,1},{1,0},{2,3},{3,2},{4,5},{5,4},{6,7},{7,6},{8,9},{9,8},{10,11... | collective-permute-start | bytes 344072 | tf_op jit(solution)/shard_map/ppermute | solution.py:106
  43.8 3.5 %collective-permute-start.29 = (bf16[8,3584]{1,0:T(8,128)(2,1)S(1)}, bf16[8,3584]{1,0:T(8,128)(2,1)S(1)}, u32[]{:S(2)}, u32[]{:S(2)}) collective-permute-start(bf16[8,3584]{1,0:T(8,128)(2,1)S(1)} %get-tuple-element.36), channel_id=1, source_target_pairs={{0,2},{1,3},{4,0},{5,1},{8,4},{9,5},{12,8},{13,9},{14,12},{15,13},... | collective-permute-start | bytes 172040 | tf_op jit(solution)/shard_map/ppermute | solution.py:106
  47.3 3.7 %collective-permute-start.30 = (bf16[8,7168]{1,0:T(8,128)(2,1)S(1)}, bf16[8,7168]{1,0:T(8,128)(2,1)S(1)}, u32[]{:S(2)}, u32[]{:S(2)}) collective-permute-start(bf16[8,7168]{1,0:T(8,128)(2,1)S(1)} %pad_maximum_fusion.1), channel_id=1, source_target_pairs={{0,2},{1,3},{4,0},{5,1},{8,4},{9,5},{12,8},{13,9},{14,12},{15,13},... | collective-permute-start | bytes 344072 | tf_op jit(solution)/shard_map/ppermute | solution.py:106
  47.4 7.4 %collective-permute-start.26 = (bf16[8,7168]{1,0:T(8,128)(2,1)S(1)}, bf16[8,7168]{1,0:T(8,128)(2,1)S(1)}, u32[]{:S(2)}, u32[]{:S(2)}) collective-permute-start(bf16[8,7168]{1,0:T(8,128)(2,1)S(1)} %get-tuple-element.24), channel_id=1, source_target_pairs={{0,1},{1,0},{2,3},{3,2},{4,5},{5,4},{6,7},{7,6},{8,9},{9,8},{10,11... | collective-permute-start | bytes 344072 | tf_op jit(solution)/shard_map/ppermute | solution.py:106
  51.1 3.7 %collective-permute-start.31 = (bf16[8,7168]{1,0:T(8,128)(2,1)S(1)}, bf16[8,7168]{1,0:T(8,128)(2,1)S(1)}, u32[]{:S(2)}, u32[]{:S(2)}) collective-permute-start(bf16[8,7168]{1,0:T(8,128)(2,1)S(1)} %fusion.21), channel_id=1, source_target_pairs={{0,2},{1,3},{4,0},{5,1},{8,4},{9,5},{12,8},{13,9},{14,12},{15,13},... | collective-permute-start | bytes 344072 | tf_op jit(solution)/shard_map/ppermute | solution.py:106
  51.2 4.1 %collective-permute-start.17 = (bf16[8,7168]{1,0:T(8,128)(2,1)S(1)}, bf16[8,7168]{1,0:T(8,128)(2,1)S(1)}, u32[]{:S(2)}, u32[]{:S(2)}) collective-permute-start(bf16[8,7168]{1,0:T(8,128)(2,1)S(1)} %get-tuple-element.21), channel_id=1, source_target_pairs={{0,1},{1,0},{2,3},{3,2},{4,5},{5,4},{6,7},{7,6},{8,9},{9,8},{10,11... | collective-permute-start | bytes 344072 | tf_op jit(solution)/shard_map/ppermute | solution.py:106
  53.6 4.8 %collective-permute-start.25 = (bf16[8,7168]{1,0:T(8,128)(2,1)S(1)}, bf16[8,7168]{1,0:T(8,128)(2,1)S(1)}, u32[]{:S(2)}, u32[]{:S(2)}) collective-permute-start(bf16[8,7168]{1,0:T(8,128)(2,1)S(1)} %get-tuple-element.29), channel_id=1, source_target_pairs={{0,4},{1,5},{4,8},{5,9},{8,12},{9,13},{12,14},{13,15},{14,10},{15,... | collective-permute-start | bytes 344072 | tf_op jit(solution)/shard_map/ppermute | solution.py:106
  54.9 3.9 %collective-permute-start.32 = (bf16[8,7168]{1,0:T(8,128)(2,1)S(1)}, bf16[8,7168]{1,0:T(8,128)(2,1)S(1)}, u32[]{:S(2)}, u32[]{:S(2)}) collective-permute-start(bf16[8,7168]{1,0:T(8,128)(2,1)S(1)} %fusion.23), channel_id=1, source_target_pairs={{0,2},{1,3},{4,0},{5,1},{8,4},{9,5},{12,8},{13,9},{14,12},{15,13},... | collective-permute-start | bytes 344072 | tf_op jit(solution)/shard_map/ppermute | solution.py:106
  59.3 6.1 %collective-permute-start.34 = (bf16[8,7168]{1,0:T(8,128)(2,1)S(1)}, bf16[8,7168]{1,0:T(8,128)(2,1)S(1)}, u32[]{:S(2)}, u32[]{:S(2)}) collective-permute-start(bf16[8,7168]{1,0:T(8,128)(2,1)S(1)} %get-tuple-element.6), channel_id=1, source_target_pairs={{0,4},{1,5},{4,8},{5,9},{8,12},{9,13},{12,14},{13,15},{14,10},{15,... | collective-permute-start | bytes 344072 | tf_op jit(solution)/shard_map/ppermute | solution.py:106
  60.6 8.9 %collective-permute-start.36 = (bf16[8,7168]{1,0:T(8,128)(2,1)S(1)}, bf16[8,7168]{1,0:T(8,128)(2,1)S(1)}, u32[]{:S(2)}, u32[]{:S(2)}) collective-permute-start(bf16[8,7168]{1,0:T(8,128)(2,1)S(1)} %get-tuple-element.6), channel_id=1, source_target_pairs={{0,2},{1,3},{4,0},{5,1},{8,4},{9,5},{12,8},{13,9},{14,12},{15,13},... | collective-permute-start | bytes 344072 | tf_op jit(solution)/shard_map/ppermute | solution.py:106
  60.8 9.1 %collective-permute-start.33 = (bf16[8,7168]{1,0:T(8,128)(2,1)S(1)}, bf16[8,7168]{1,0:T(8,128)(2,1)S(1)}, u32[]{:S(2)}, u32[]{:S(2)}) collective-permute-start(bf16[8,7168]{1,0:T(8,128)(2,1)S(1)} %get-tuple-element.6), channel_id=1, source_target_pairs={{0,1},{1,0},{2,3},{3,2},{4,5},{5,4},{6,7},{7,6},{8,9},{9,8},{10,11... | collective-permute-start | bytes 344072 | tf_op jit(solution)/shard_map/ppermute | solution.py:106
  65.4 9.9 %collective-permute-start.35 = (bf16[8,7168]{1,0:T(8,128)(2,1)S(1)}, bf16[8,7168]{1,0:T(8,128)(2,1)S(1)}, u32[]{:S(2)}, u32[]{:S(2)}) collective-permute-start(bf16[8,7168]{1,0:T(8,128)(2,1)S(1)} %collective-permute-done.34), channel_id=1, source_target_pairs={{0,1},{1,0},{2,3},{3,2},{4,5},{5,4},{6,7},{7,6},{8,9},{9,8},{10,11... | collective-permute-start | bytes 344072 | tf_op jit(solution)/shard_map/ppermute | solution.py:106
  68.2 4.8 %collective-permute-start.38 = (bf16[8,7168]{1,0:T(8,128)(2,1)S(1)}, bf16[8,7168]{1,0:T(8,128)(2,1)S(1)}, u32[]{:S(2)}, u32[]{:S(2)}) collective-permute-start(bf16[8,7168]{1,0:T(8,128)(2,1)S(1)} %collective-permute-done.34), channel_id=1, source_target_pairs={{0,4},{1,5},{4,8},{5,9},{8,12},{9,13},{12,14},{13,15},{14,10},{15,... | collective-permute-start | bytes 344072 | tf_op jit(solution)/shard_map/ppermute | solution.py:106
  69.5 6.0 %collective-permute-start.37 = (bf16[8,7168]{1,0:T(8,128)(2,1)S(1)}, bf16[8,7168]{1,0:T(8,128)(2,1)S(1)}, u32[]{:S(2)}, u32[]{:S(2)}) collective-permute-start(bf16[8,7168]{1,0:T(8,128)(2,1)S(1)} %collective-permute-done.36), channel_id=1, source_target_pairs={{0,1},{1,0},{2,3},{3,2},{4,5},{5,4},{6,7},{7,6},{8,9},{9,8},{10,11... | collective-permute-start | bytes 344072 | tf_op jit(solution)/shard_map/ppermute | solution.py:106
  69.8 5.3 %collective-permute-start.40 = (bf16[8,7168]{1,0:T(8,128)(2,1)S(1)}, bf16[8,7168]{1,0:T(8,128)(2,1)S(1)}, u32[]{:S(2)}, u32[]{:S(2)}) collective-permute-start(bf16[8,7168]{1,0:T(8,128)(2,1)S(1)} %collective-permute-done.36), channel_id=1, source_target_pairs={{0,2},{1,3},{4,0},{5,1},{8,4},{9,5},{12,8},{13,9},{14,12},{15,13},... | collective-permute-start | bytes 344072 | tf_op jit(solution)/shard_map/ppermute | solution.py:106
  73.0 10.0 %collective-permute-start.39 = (bf16[8,7168]{1,0:T(8,128)(2,1)S(1)}, bf16[8,7168]{1,0:T(8,128)(2,1)S(1)}, u32[]{:S(2)}, u32[]{:S(2)}) collective-permute-start(bf16[8,7168]{1,0:T(8,128)(2,1)S(1)} %collective-permute-done.38), channel_id=1, source_target_pairs={{0,1},{1,0},{2,3},{3,2},{4,5},{5,4},{6,7},{7,6},{8,9},{9,8},{10,11... | collective-permute-start | bytes 344072 | tf_op jit(solution)/shard_map/ppermute | solution.py:106
  73.7 6.3 %collective-permute-start.42 = (bf16[8,7168]{1,0:T(8,128)(2,1)S(1)}, bf16[8,7168]{1,0:T(8,128)(2,1)S(1)}, u32[]{:S(2)}, u32[]{:S(2)}) collective-permute-start(bf16[8,7168]{1,0:T(8,128)(2,1)S(1)} %collective-permute-done.38), channel_id=1, source_target_pairs={{0,4},{1,5},{4,8},{5,9},{8,12},{9,13},{12,14},{13,15},{14,10},{15,... | collective-permute-start | bytes 344072 | tf_op jit(solution)/shard_map/ppermute | solution.py:106
  75.0 8.0 %collective-permute-start.41 = (bf16[8,7168]{1,0:T(8,128)(2,1)S(1)}, bf16[8,7168]{1,0:T(8,128)(2,1)S(1)}, u32[]{:S(2)}, u32[]{:S(2)}) collective-permute-start(bf16[8,7168]{1,0:T(8,128)(2,1)S(1)} %collective-permute-done.40), channel_id=1, source_target_pairs={{0,1},{1,0},{2,3},{3,2},{4,5},{5,4},{6,7},{7,6},{8,9},{9,8},{10,11... | collective-permute-start | bytes 344072 | tf_op jit(solution)/shard_map/ppermute | solution.py:106
  75.3 4.5 %collective-permute-start.44 = (bf16[8,7168]{1,0:T(8,128)(2,1)S(1)}, bf16[8,7168]{1,0:T(8,128)(2,1)S(1)}, u32[]{:S(2)}, u32[]{:S(2)}) collective-permute-start(bf16[8,7168]{1,0:T(8,128)(2,1)S(1)} %collective-permute-done.40), channel_id=1, source_target_pairs={{0,2},{1,3},{4,0},{5,1},{8,4},{9,5},{12,8},{13,9},{14,12},{15,13},... | collective-permute-start | bytes 344072 | tf_op jit(solution)/shard_map/ppermute | solution.py:106
  79.9 3.2 %collective-permute-start.47 = (bf16[8,3584]{1,0:T(8,128)(2,1)S(1)}, bf16[8,3584]{1,0:T(8,128)(2,1)S(1)}, u32[]{:S(2)}, u32[]{:S(2)}) collective-permute-start(bf16[8,3584]{1,0:T(8,128)(2,1)S(1)} %slice.221), channel_id=1, source_target_pairs={{0,2},{1,3},{4,0},{5,1},{8,4},{9,5},{12,8},{13,9},{14,12},{15,13},... | collective-permute-start | bytes 172040 | tf_op jit(solution)/shard_map/ppermute | solution.py:106
  80.0 5.0 %collective-permute-start.46 = (bf16[8,3584]{1,0:T(8,128)(2,1)S(1)}, bf16[8,3584]{1,0:T(8,128)(2,1)S(1)}, u32[]{:S(2)}, u32[]{:S(2)}) collective-permute-start(bf16[8,3584]{1,0:T(8,128)(2,1)S(1)} %slice.220), channel_id=1, source_target_pairs={{0,4},{1,5},{4,8},{5,9},{8,12},{9,13},{12,14},{13,15},{14,10},{15,... | collective-permute-start | bytes 172040 | tf_op jit(solution)/shard_map/ppermute | solution.py:106
  81.4 4.2 %collective-permute-start.43 = (bf16[8,7168]{1,0:T(8,128)(2,1)S(1)}, bf16[8,7168]{1,0:T(8,128)(2,1)S(1)}, u32[]{:S(2)}, u32[]{:S(2)}) collective-permute-start(bf16[8,7168]{1,0:T(8,128)(2,1)S(1)} %collective-permute-done.42), channel_id=1, source_target_pairs={{0,1},{1,0},{2,3},{3,2},{4,5},{5,4},{6,7},{7,6},{8,9},{9,8},{10,11... | collective-permute-start | bytes 344072 | tf_op jit(solution)/shard_map/ppermute | solution.py:106
  83.0 2.6 %collective-permute-start.45 = (bf16[8,7168]{1,0:T(8,128)(2,1)S(1)}, bf16[8,7168]{1,0:T(8,128)(2,1)S(1)}, u32[]{:S(2)}, u32[]{:S(2)}) collective-permute-start(bf16[8,7168]{1,0:T(8,128)(2,1)S(1)} %collective-permute-done.44), channel_id=1, source_target_pairs={{0,1},{1,0},{2,3},{3,2},{4,5},{5,4},{6,7},{7,6},{8,9},{9,8},{10,11... | collective-permute-start | bytes 344072 | tf_op jit(solution)/shard_map/ppermute | solution.py:106
  83.1 2.9 %collective-permute-start.49 = (bf16[8,3584]{1,0:T(8,128)(2,1)S(1)}, bf16[8,3584]{1,0:T(8,128)(2,1)S(1)}, u32[]{:S(2)}, u32[]{:S(2)}) collective-permute-start(bf16[8,3584]{1,0:T(8,128)(2,1)S(1)} %collective-permute-done.47), channel_id=1, source_target_pairs={{0,1},{1,0},{2,3},{3,2},{4,5},{5,4},{6,7},{7,6},{8,9},{9,8},{10,11... | collective-permute-start | bytes 172040 | tf_op jit(solution)/shard_map/ppermute | solution.py:106
  85.1 1.4 %collective-permute-start.48 = (bf16[8,3584]{1,0:T(8,128)(2,1)S(1)}, bf16[8,3584]{1,0:T(8,128)(2,1)S(1)}, u32[]{:S(2)}, u32[]{:S(2)}) collective-permute-start(bf16[8,3584]{1,0:T(8,128)(2,1)S(1)} %collective-permute-done.46), channel_id=1, source_target_pairs={{0,1},{1,0},{2,3},{3,2},{4,5},{5,4},{6,7},{7,6},{8,9},{9,8},{10,11... | collective-permute-start | bytes 172040 | tf_op jit(solution)/shard_map/ppermute | solution.py:106
  88.5 1.4 %collective-permute-start.53 = (bf16[8,7168]{1,0:T(8,128)(2,1)S(1)}, bf16[8,7168]{1,0:T(8,128)(2,1)S(1)}, u32[]{:S(2)}, u32[]{:S(2)}) collective-permute-start(bf16[8,7168]{1,0:T(8,128)(2,1)S(1)} %get-tuple-element.14), channel_id=1, source_target_pairs={{0,1},{1,0},{2,3},{3,2},{4,5},{5,4},{6,7},{7,6},{8,9},{9,8},{10,11... | collective-permute-start | bytes 344072 | tf_op jit(solution)/shard_map/ppermute | solution.py:106
  90.3 3.1 %collective-permute-start.55 = (bf16[8,3584]{1,0:T(8,128)(2,1)S(1)}, bf16[8,3584]{1,0:T(8,128)(2,1)S(1)}, u32[]{:S(2)}, u32[]{:S(2)}) collective-permute-start(bf16[8,3584]{1,0:T(8,128)(2,1)S(1)} %get-tuple-element.33), channel_id=1, source_target_pairs={{0,4},{1,5},{4,8},{5,9},{8,12},{9,13},{12,14},{13,15},{14,10},{15,... | collective-permute-start | bytes 172040 | tf_op jit(solution)/shard_map/ppermute | solution.py:106
  91.7 4.7 %collective-permute-start.52 = (bf16[8,7168]{1,0:T(8,128)(2,1)S(1)}, bf16[8,7168]{1,0:T(8,128)(2,1)S(1)}, u32[]{:S(2)}, u32[]{:S(2)}) collective-permute-start(bf16[8,7168]{1,0:T(8,128)(2,1)S(1)} %get-tuple-element.15), channel_id=1, source_target_pairs={{0,1},{1,0},{2,3},{3,2},{4,5},{5,4},{6,7},{7,6},{8,9},{9,8},{10,11... | collective-permute-start | bytes 344072 | tf_op jit(solution)/shard_map/ppermute | solution.py:106
  93.4 3.7 %collective-permute-start.56 = (bf16[8,7168]{1,0:T(8,128)(2,1)S(1)}, bf16[8,7168]{1,0:T(8,128)(2,1)S(1)}, u32[]{:S(2)}, u32[]{:S(2)}) collective-permute-start(bf16[8,7168]{1,0:T(8,128)(2,1)S(1)} %pad_maximum_fusion.2), channel_id=1, source_target_pairs={{0,4},{1,5},{4,8},{5,9},{8,12},{9,13},{12,14},{13,15},{14,10},{15,... | collective-permute-start | bytes 344072 | tf_op jit(solution)/shard_map/ppermute | solution.py:106
  94.8 6.7 %collective-permute-start.51 = (bf16[8,7168]{1,0:T(8,128)(2,1)S(1)}, bf16[8,7168]{1,0:T(8,128)(2,1)S(1)}, u32[]{:S(2)}, u32[]{:S(2)}) collective-permute-start(bf16[8,7168]{1,0:T(8,128)(2,1)S(1)} %get-tuple-element.16), channel_id=1, source_target_pairs={{0,1},{1,0},{2,3},{3,2},{4,5},{5,4},{6,7},{7,6},{8,9},{9,8},{10,11... | collective-permute-start | bytes 344072 | tf_op jit(solution)/shard_map/ppermute | solution.py:106
  96.4 5.1 %collective-permute-start.61 = (bf16[8,7168]{1,0:T(8,128)(2,1)S(1)}, bf16[8,7168]{1,0:T(8,128)(2,1)S(1)}, u32[]{:S(2)}, u32[]{:S(2)}) collective-permute-start(bf16[8,7168]{1,0:T(8,128)(2,1)S(1)} %get-tuple-element.10), channel_id=1, source_target_pairs={{0,1},{1,0},{2,3},{3,2},{4,5},{5,4},{6,7},{7,6},{8,9},{9,8},{10,11... | collective-permute-start | bytes 344072 | tf_op jit(solution)/shard_map/ppermute | solution.py:106
  97.2 4.3 %collective-permute-start.57 = (bf16[8,7168]{1,0:T(8,128)(2,1)S(1)}, bf16[8,7168]{1,0:T(8,128)(2,1)S(1)}, u32[]{:S(2)}, u32[]{:S(2)}) collective-permute-start(bf16[8,7168]{1,0:T(8,128)(2,1)S(1)} %fusion.14), channel_id=1, source_target_pairs={{0,4},{1,5},{4,8},{5,9},{8,12},{9,13},{12,14},{13,15},{14,10},{15,... | collective-permute-start | bytes 344072 | tf_op jit(solution)/shard_map/ppermute | solution.py:106
  98.5 7.8 %collective-permute-start.60 = (bf16[8,7168]{1,0:T(8,128)(2,1)S(1)}, bf16[8,7168]{1,0:T(8,128)(2,1)S(1)}, u32[]{:S(2)}, u32[]{:S(2)}) collective-permute-start(bf16[8,7168]{1,0:T(8,128)(2,1)S(1)} %get-tuple-element.11), channel_id=1, source_target_pairs={{0,1},{1,0},{2,3},{3,2},{4,5},{5,4},{6,7},{7,6},{8,9},{9,8},{10,11... | collective-permute-start | bytes 344072 | tf_op jit(solution)/shard_map/ppermute | solution.py:106
  101.3 3.5 %collective-permute-start.62 = (bf16[8,3584]{1,0:T(8,128)(2,1)S(1)}, bf16[8,3584]{1,0:T(8,128)(2,1)S(1)}, u32[]{:S(2)}, u32[]{:S(2)}) collective-permute-start(bf16[8,3584]{1,0:T(8,128)(2,1)S(1)} %get-tuple-element.34), channel_id=1, source_target_pairs={{0,2},{1,3},{4,0},{5,1},{8,4},{9,5},{12,8},{13,9},{14,12},{15,13},... | collective-permute-start | bytes 172040 | tf_op jit(solution)/shard_map/ppermute | solution.py:106
  104.9 3.7 %collective-permute-start.63 = (bf16[8,7168]{1,0:T(8,128)(2,1)S(1)}, bf16[8,7168]{1,0:T(8,128)(2,1)S(1)}, u32[]{:S(2)}, u32[]{:S(2)}) collective-permute-start(bf16[8,7168]{1,0:T(8,128)(2,1)S(1)} %pad_maximum_fusion.3), channel_id=1, source_target_pairs={{0,2},{1,3},{4,0},{5,1},{8,4},{9,5},{12,8},{13,9},{14,12},{15,13},... | collective-permute-start | bytes 344072 | tf_op jit(solution)/shard_map/ppermute | solution.py:106
  105.2 9.1 %collective-permute-start.59 = (bf16[8,7168]{1,0:T(8,128)(2,1)S(1)}, bf16[8,7168]{1,0:T(8,128)(2,1)S(1)}, u32[]{:S(2)}, u32[]{:S(2)}) collective-permute-start(bf16[8,7168]{1,0:T(8,128)(2,1)S(1)} %get-tuple-element.12), channel_id=1, source_target_pairs={{0,1},{1,0},{2,3},{3,2},{4,5},{5,4},{6,7},{7,6},{8,9},{9,8},{10,11... | collective-permute-start | bytes 344072 | tf_op jit(solution)/shard_map/ppermute | solution.py:106
  108.6 5.7 %collective-permute-start.64 = (bf16[8,7168]{1,0:T(8,128)(2,1)S(1)}, bf16[8,7168]{1,0:T(8,128)(2,1)S(1)}, u32[]{:S(2)}, u32[]{:S(2)}) collective-permute-start(bf16[8,7168]{1,0:T(8,128)(2,1)S(1)} %fusion.9), channel_id=1, source_target_pairs={{0,2},{1,3},{4,0},{5,1},{8,4},{9,5},{12,8},{13,9},{14,12},{15,13},... | collective-permute-start | bytes 344072 | tf_op jit(solution)/shard_map/ppermute | solution.py:106
  110.7 4.4 %collective-permute-start.50 = (bf16[8,7168]{1,0:T(8,128)(2,1)S(1)}, bf16[8,7168]{1,0:T(8,128)(2,1)S(1)}, u32[]{:S(2)}, u32[]{:S(2)}) collective-permute-start(bf16[8,7168]{1,0:T(8,128)(2,1)S(1)} %get-tuple-element.9), channel_id=1, source_target_pairs={{0,1},{1,0},{2,3},{3,2},{4,5},{5,4},{6,7},{7,6},{8,9},{9,8},{10,11... | collective-permute-start | bytes 344072 | tf_op jit(solution)/shard_map/ppermute | solution.py:106
  113.0 4.8 %collective-permute-start.58 = (bf16[8,7168]{1,0:T(8,128)(2,1)S(1)}, bf16[8,7168]{1,0:T(8,128)(2,1)S(1)}, u32[]{:S(2)}, u32[]{:S(2)}) collective-permute-start(bf16[8,7168]{1,0:T(8,128)(2,1)S(1)} %get-tuple-element.17), channel_id=1, source_target_pairs={{0,4},{1,5},{4,8},{5,9},{8,12},{9,13},{12,14},{13,15},{14,10},{15,... | collective-permute-start | bytes 344072 | tf_op jit(solution)/shard_map/ppermute | solution.py:106
  114.3 3.8 %collective-permute-start.65 = (bf16[8,7168]{1,0:T(8,128)(2,1)S(1)}, bf16[8,7168]{1,0:T(8,128)(2,1)S(1)}, u32[]{:S(2)}, u32[]{:S(2)}) collective-permute-start(bf16[8,7168]{1,0:T(8,128)(2,1)S(1)} %fusion.11), channel_id=1, source_target_pairs={{0,2},{1,3},{4,0},{5,1},{8,4},{9,5},{12,8},{13,9},{14,12},{15,13},... | collective-permute-start | bytes 344072 | tf_op jit(solution)/shard_map/ppermute | solution.py:106
  (7 other events, 49.8 us)
